TPU v7x, 32 devices: a whole 2x2x4 slice. The times are simulated.
32 devices in a mesh: section: 4 (over x, core), ep: 8 (over z, y).
Axes of the slice: x: 2, y: 2, z: 4, core: 2. Of those that a mesh axis runs over, the one named last changes fastest.
Arguments:
- tokens: bfloat16 [2048, 1440], P('ep', 'section'), may hold values from -6 to 6
- grad_out: bfloat16 [2048, 1440], P('ep', 'section'), may hold values from -6 to 6
- expert_ids: int32 [2048, 4], P('ep'), may hold values from 0 to 7, all different within a row; in each aligned block of 256 rows (0 to 255, 256 to 511, ...) at most 192 rows name the same one
- probs: float32 [2048, 4], P('ep'), may hold values from 0.05 to 1
- w_gate: bfloat16 [8, 1440, 2880], P('ep', None, 'section'), may hold values from -0.15625 to 0.15625
- w_up: bfloat16 [8, 1440, 2880], P('ep', None, 'section'), may hold values from -0.15625 to 0.15625
- w_down: bfloat16 [8, 2880, 1440], P('ep', 'section'), may hold values from -0.109375 to 0.109375
Outputs:
- grad_gate: bfloat16 [8, 1440, 2880], P('ep', None, 'section')
- grad_up: bfloat16 [8, 1440, 2880], P('ep', None, 'section')
- grad_down: bfloat16 [8, 2880, 1440], P('ep', 'section')
Inputs may be any that keep to these rules, and one draw needn't show every extreme that they name: `expert_ids`: among the picks of the 256 tokens of one index of ep, no expert is named more than 192 times, and the 4 experts of a token differ.
All inputs are finite; a program needn't handle non-finite values.
Results may differ from a plain program's by a relative error of at most 0.0065.
Values may be sent and summed in bfloat16 or wider, within the bound.
A program may use at most 128 MiB of HBM per device.

v0:
```python
import jax
import jax.numpy as jnp
from jax import lax
from jax.experimental import pallas as pl
from jax.experimental.pallas import tpu as pltpu
from jax.sharding import PartitionSpec as P


def rounded(value):
    return lax.optimization_barrier(value.astype(jnp.bfloat16)).astype(jnp.float32)


def slot_grads(inputs, scaled, gate_w, up_w, down_w):
    gate = jnp.einsum("hpscd,sdf->hpscf", inputs, gate_w, preferred_element_type=jnp.float32)
    linear = jnp.einsum("hpscd,sdf->hpscf", inputs, up_w, preferred_element_type=jnp.float32)
    sigma = jax.nn.sigmoid(gate)
    hidden = (gate * sigma * linear).astype(jnp.bfloat16)
    grad_hidden = jnp.einsum("hpscd,sfd->hpscf", scaled, down_w, preferred_element_type=jnp.float32)
    gate_term = (grad_hidden * linear * sigma * (1.0 + gate * (1.0 - sigma))).astype(jnp.bfloat16)
    linear_term = (grad_hidden * gate * sigma).astype(jnp.bfloat16)
    part_gate = rounded(
        jnp.einsum("hpscd,hpscf->hsdf", inputs, gate_term, preferred_element_type=jnp.float32)
    )
    part_up = rounded(
        jnp.einsum("hpscd,hpscf->hsdf", inputs, linear_term, preferred_element_type=jnp.float32)
    )
    part_down = rounded(
        jnp.einsum("hpscf,hpscd->hsfd", hidden, scaled, preferred_element_type=jnp.float32)
    )
    return (part_gate, part_up, part_down)


def shards(tokens, grad_out, expert_ids, probs, w_gate, w_up, w_down):
    n_ep = lax.axis_size("ep")
    half = n_ep // 2
    tok_dev, top = expert_ids.shape
    picks = tok_dev * top
    capacity = max(2, (3 * picks + 2 * n_ep - 1) // (2 * n_ep))
    flat_ids = expert_ids.reshape(picks)
    owners = jnp.arange(n_ep, dtype=jnp.int32)
    slots = 1
    matches = (flat_ids[:, None] == owners[None, :]).astype(jnp.int32)
    rank = jnp.sum(jnp.cumsum(matches, axis=0) * matches, axis=1) - 1
    position = flat_ids * slots * capacity + rank
    width = tokens.shape[1]
    rows = jnp.repeat(tokens, top, axis=0)
    scaled = (
        probs.reshape(picks, 1) * jnp.repeat(grad_out, top, axis=0).astype(jnp.float32)
    ).astype(jnp.bfloat16)
    buffer_rows = n_ep * slots * capacity
    send_rows = jnp.zeros((buffer_rows, width), jnp.bfloat16).at[position].set(rows)
    send_scaled = jnp.zeros((buffer_rows, width), jnp.bfloat16).at[position].set(scaled)
    send_rows = send_rows.reshape(n_ep, slots * capacity, width)
    send_scaled = send_scaled.reshape(n_ep, slots * capacity, width)
    got_rows, got_scaled = (
        lax.all_to_all(send_rows, "ep", split_axis=0, concat_axis=0, tiled=True),
        lax.all_to_all(send_scaled, "ep", split_axis=0, concat_axis=0, tiled=True),
    )
    got_rows = got_rows.reshape(2, half, slots, capacity, width)
    got_scaled = got_scaled.reshape(2, half, slots, capacity, width)
    inputs, scaled_rows = (
        lax.all_gather(got_rows, "section", axis=4, tiled=True),
        lax.all_gather(got_scaled, "section", axis=4, tiled=True),
    )
    part_gate, part_up, part_down = slot_grads(inputs, scaled_rows, w_gate, w_up, w_down)
    grad_gate = (part_gate[0] + part_gate[1]).astype(jnp.bfloat16)
    grad_up = (part_up[0] + part_up[1]).astype(jnp.bfloat16)
    grad_down = (part_down[0] + part_down[1]).astype(jnp.bfloat16)
    return (grad_gate, grad_up, grad_down)


MESH = pl.DeviceIdType.MESH
TILE = 256


def fused_kernel(
    tokens, grad_out, ids, probs, w_gate, w_up, w_down,
    out_gate, out_up, out_down,
    held, wg, wu, wd, wg_t, wu_t, acc_gate, acc_up, acc_down, cols_in, cols_scaled, term_gate, term_linear, term_hidden,
    w_sem, z_send, z_recv, x_send, x_recv, y_send, y_recv, dx_send, dx_recv, dy_send, dy_recv, c_send, c_recv, d_send, d_recv,
):
    sec, me = lax.axis_index("section"), lax.axis_index("ep")
    width, n_tok = tokens.shape
    n_sec = held.shape[1]
    feats, units = w_gate.shape
    z, y = me // 2, me % 2
    h = z // 2
    zz = z + h * (3 - 2 * z)
    x_peer = (sec + 2) % 4
    core_peer = sec + 1 - 2 * (sec % 2)
    y_peer = me + 1 - 2 * y
    inward = me + 2 - 4 * h
    outward = me - 2 + 4 * h
    block_rows = held.shape[2]
    half = block_rows // 2
    side = block_rows // 5 // 16 * 16
    along = block_rows - 2 * side

    loads = [
        pltpu.make_async_copy(src, dst, w_sem.at[i])
        for i, (src, dst) in enumerate(((w_gate, wg), (w_up, wu), (w_down, wd)))
    ]
    for load in loads:
        load.start()

    barrier = pltpu.get_barrier_semaphore()

    def greet(**where):
        pl.semaphore_signal(barrier, inc=1, device_id=where, device_id_type=MESH)

    greet(section=x_peer)
    greet(section=core_peer)
    greet(ep=y_peer)
    greet(ep=inward)

    @pl.when(zz == 1)
    def _():
        greet(ep=outward)

    own = held.at[me, sec]
    own[:width, :] = tokens[...]
    own[width : 2 * width, :] = grad_out[...]
    n_ep = held.shape[0]
    expert = lax.broadcasted_iota(jnp.int32, (n_ep, n_tok), 0)
    weight = jnp.zeros((n_ep, n_tok), jnp.float32)
    for k in range(ids.shape[0]):
        weight = weight + jnp.where(ids[k : k + 1, :] == expert, probs[k : k + 1, :], 0.0)
    high = weight.astype(jnp.bfloat16).astype(jnp.float32)
    own[2 * width :, :] = jnp.concatenate([high, weight - high], axis=0).astype(jnp.bfloat16)

    @pl.when(zz == 0)
    def _():
        pl.semaphore_wait(barrier, 4)

    @pl.when(zz == 1)
    def _():
        pl.semaphore_wait(barrier, 5)

    def send(block, send_sem, recv_sem, **where):
        return pltpu.make_async_remote_copy(
            src_ref=block, dst_ref=block, send_sem=send_sem, recv_sem=recv_sem,
            device_id=where, device_id_type=MESH,
        )

    def source(k):
        s = k + (1 - k // 2) * ((k + zz) % 2 - k % 2)
        return s + h * (3 - 2 * s)

    def mine(k):
        return 2 * source(k) + y

    def other(k):
        return 2 * source(k) + 1 - y

    def upper(block, first):
        return block.at[pl.ds(0, half)] if first else block.at[pl.ds(along, side)]

    def lower(block, first):
        return block.at[pl.ds(half, half)] if first else block.at[pl.ds(along + side, side)]

    def d_block(k):
        return held.at[other(k), x_peer, pl.ds(0, along)]

    def d_in(k, idx):
        return send(d_block(k), d_send.at[0, idx], d_recv.at[idx], ep=inward)

    def d_out(k, idx):
        return send(d_block(k), d_send.at[1, idx], d_recv.at[idx], ep=outward)

    def d_arrived(k):
        send(d_block(k), d_send.at[0, k], d_recv.at[k], ep=inward).wait_recv()

    def z_arrived(k):
        send(held.at[mine(k), sec], z_send.at[0, k], z_recv.at[k], ep=inward).wait_recv()

    def z_in(k, idx):
        return send(held.at[mine(k), sec], z_send.at[0, idx], z_recv.at[idx], ep=inward)

    def z_out(k, idx):
        return send(held.at[mine(k), sec], z_send.at[1, idx], z_recv.at[idx], ep=outward)

    def x_whole(k):
        return send(held.at[mine(k), sec], x_send.at[k], x_recv.at[k], section=x_peer)

    def y_whole(k):
        return send(held.at[mine(k), sec], y_send.at[k], y_recv.at[k], ep=y_peer)

    def x_half(k, first):
        return send(upper(held.at[other(k), sec], first), dx_send.at[k], dx_recv.at[k], section=x_peer)

    def y_half(k, first):
        return send(lower(held.at[mine(k), x_peer], first), dy_send.at[k], dy_recv.at[k], ep=y_peer)

    def by_step(k, act):
        @pl.when(k == 0)
        def _():
            act(True)

        @pl.when(k > 0)
        def _():
            act(False)

    def core(k, which):
        block = held.at[mine(k) if which < 2 else other(k), sec if which % 2 == 0 else x_peer]
        return send(block, c_send.at[k, which], c_recv.at[k, which], section=core_peer)

    def x_arrived(k):
        send(held.at[mine(k), x_peer], x_send.at[k], x_recv.at[k], section=x_peer).wait_recv()

    def y_arrived(k):
        send(held.at[other(k), sec], y_send.at[k], y_recv.at[k], ep=y_peer).wait_recv()

    def diagonal_arrived(k):
        block = held.at[other(k), x_peer]

        def sides(first):
            send(upper(block, first), dx_send.at[k], dx_recv.at[k], section=x_peer).wait_recv()
            send(lower(block, first), dy_send.at[k], dy_recv.at[k], ep=y_peer).wait_recv()

        by_step(k, sides)

        @pl.when((zz == 0) & (k > 0))
        def _():
            d_arrived(k)

    def core_arrived(k, which):
        block = held.at[
            mine(k) if which < 2 else other(k),
            core_peer if which % 2 == 0 else (core_peer + 2) % 4,
        ]
        send(block, c_send.at[k, which], c_recv.at[k, which], section=core_peer).wait_recv()

    def column(k):
        x_whole(k).start()
        y_whole(k).start()
        core(k, 0).start()

    def forward(slot, at):
        here = pl.ds(at, n_tok)
        block = held.at[slot]
        parts = block[0, 2 * width :, :].astype(jnp.float32)
        which = lax.broadcasted_iota(jnp.int32, parts.shape, 0) % n_ep
        weight = jnp.sum(jnp.where(which == me, parts, 0.0), axis=0, keepdims=True)
        for s in range(n_sec):
            part = pl.ds(s * width, width)
            cols_in[part, here] = block[s, :width, :]
            cot = block[s, width : 2 * width, :].astype(jnp.float32)
            cols_scaled[part, here] = (weight * cot).astype(jnp.bfloat16)
        gate = jnp.dot(wg_t[...], cols_in[:, here], preferred_element_type=jnp.float32)
        linear = jnp.dot(wu_t[...], cols_in[:, here], preferred_element_type=jnp.float32)
        grad = jnp.dot(wd[...], cols_scaled[:, here], preferred_element_type=jnp.float32)
        sigma = jax.nn.sigmoid(gate)
        silu = gate * sigma
        term_hidden[:, here] = (silu * linear).astype(jnp.bfloat16)
        term_gate[:, here] = (grad * linear * sigma * (1.0 + gate * (1.0 - sigma))).astype(jnp.bfloat16)
        term_linear[:, here] = (grad * silu).astype(jnp.bfloat16)

    def outer(lhs, rhs):
        return lax.dot_general(lhs, rhs, (((1,), (1,)), ((), ())), preferred_element_type=jnp.float32)

    def weights():
        for at in range(0, units, TILE):
            to = min(units, at + TILE)
            acc_gate[:, at:to] += outer(cols_in[...], term_gate[at:to, :])
            acc_up[:, at:to] += outer(cols_in[...], term_linear[at:to, :])
        for at in range(0, feats, TILE):
            to = min(feats, at + TILE)
            acc_down[:, at:to] += outer(term_hidden[...], cols_scaled[at:to, :])

    z_in(0, 1 + zz).start()

    @pl.when(zz == 1)
    def _():
        z_out(0, 1).start()

    column(0)

    def clear(m, carry):
        part = feats // 6
        here = pl.ds(pl.multiple_of(m * part, 16), part)
        acc_gate[here, :] = jnp.zeros((part, units), jnp.float32)
        acc_up[here, :] = jnp.zeros((part, units), jnp.float32)
        return carry

    lax.fori_loop(0, 6, clear, 0)

    def clear_down(m, carry):
        part = units // 3
        here = pl.ds(pl.multiple_of(m * part, 16), part)
        acc_down[here, :] = jnp.zeros((part, feats), jnp.float32)
        return carry

    lax.fori_loop(0, 3, clear_down, 0)

    for load in loads:
        load.wait()
    for at in range(0, feats, TILE):
        to = min(feats, at + TILE)
        wg_t[:, at:to] = wg[at:to, :].T
        wu_t[:, at:to] = wu[at:to, :].T

    def step(k, carry):
        x_arrived(k)
        by_step(k, lambda first: y_half(k, first).start())
        core(k, 1).start()
        y_arrived(k)
        by_step(k, lambda first: x_half(k, first).start())
        core(k, 2).start()

        @pl.when(k < 3)
        def _():
            nxt = k + 1

            @pl.when((zz == 0) | (nxt == 1))
            def _():
                z_arrived(nxt)

            @pl.when((zz == 1) & (nxt == 1))
            def _():
                z_in(1, 3).start()
                z_arrived(2)
                z_out(2, 2).start()

            column(nxt)

        @pl.when((zz == 1) & (k == 1))
        def _():
            d_arrived(1)
            d_in(1, 3).start()
            d_arrived(2)
            d_out(2, 2).start()

        core_arrived(k, 0)
        core_arrived(k, 1)
        forward(mine(k), 0)
        diagonal_arrived(k)
        core(k, 3).start()

        @pl.when(k == 0)
        def _():
            d_in(0, 1 + zz).start()

            @pl.when(zz == 1)
            def _():
                d_out(0, 1).start()
                z_arrived(3)
                z_out(3, 3).start()

        core_arrived(k, 2)
        core_arrived(k, 3)
        forward(other(k), n_tok)

        @pl.when((zz == 1) & (k == 1))
        def _():
            d_arrived(3)
            d_out(3, 3).start()

        weights()
        return carry

    lax.fori_loop(0, 4, step, 0)

    def finish(m, carry):
        part = feats // 6
        here = pl.ds(pl.multiple_of(m * part, 16), part)
        out_gate[here, :] = acc_gate[here, :].astype(jnp.bfloat16)
        out_up[here, :] = acc_up[here, :].astype(jnp.bfloat16)
        return carry

    lax.fori_loop(0, 6, finish, 0)

    def finish_down(m, carry):
        part = units // 3
        here = pl.ds(pl.multiple_of(m * part, 16), part)
        out_down[here, :] = acc_down[here, :].astype(jnp.bfloat16)
        return carry

    lax.fori_loop(0, 3, finish_down, 0)

    z_in(0, 1 + zz).wait_send()
    d_in(0, 1 + zz).wait_send()

    @pl.when(zz == 1)
    def _():
        z_out(0, 1).wait_send()
        z_in(1, 3).wait_send()
        z_out(2, 2).wait_send()
        z_out(3, 3).wait_send()
        d_out(0, 1).wait_send()
        d_in(1, 3).wait_send()
        d_out(2, 2).wait_send()
        d_out(3, 3).wait_send()

    def drain(k, carry):
        x_whole(k).wait_send()
        y_whole(k).wait_send()

        def sides(first):
            x_half(k, first).wait_send()
            y_half(k, first).wait_send()

        by_step(k, sides)
        for which in range(4):
            core(k, which).wait_send()
        return carry

    lax.fori_loop(0, 4, drain, 0)


def copy_kernel(gate, up, down, out_gate, out_up, out_down):
    out_gate[...] = gate[...]
    out_up[...] = up[...]
    out_down[...] = down[...]


def fused(tokens, grad_out, expert_ids, probs, w_gate, w_up, w_down):
    n_ep, n_sec = lax.axis_size("ep"), lax.axis_size("section")
    n_tok, width = tokens.shape
    feats, units = w_gate.shape[1:]
    bf16, f32 = jnp.bfloat16, jnp.float32
    dma = pltpu.SemaphoreType.DMA
    vmem, hbm = pl.BlockSpec(memory_space=pltpu.VMEM), pl.BlockSpec(memory_space=pl.ANY)
    rows = n_ep * n_tok
    shapes = (
        jax.ShapeDtypeStruct((feats, units), bf16),
        jax.ShapeDtypeStruct((feats, units), bf16),
        jax.ShapeDtypeStruct((units, feats), bf16),
    )
    outs = pl.pallas_call(
        fused_kernel,
        out_shape=shapes,
        in_specs=[vmem] * 4 + [hbm] * 3,
        out_specs=(vmem,) * 3,
        scratch_shapes=[
            pltpu.VMEM((n_ep, n_sec, 2 * width + 2 * n_ep, n_tok), bf16),
            pltpu.VMEM((feats, units), bf16),
            pltpu.VMEM((feats, units), bf16),
            pltpu.VMEM((units, feats), bf16),
            pltpu.VMEM((units, feats), bf16),
            pltpu.VMEM((units, feats), bf16),
            pltpu.VMEM((feats, units), f32),
            pltpu.VMEM((feats, units), f32),
            pltpu.VMEM((units, feats), f32),
            pltpu.VMEM((feats, 2 * n_tok), bf16),
            pltpu.VMEM((feats, 2 * n_tok), bf16),
            pltpu.VMEM((units, 2 * n_tok), bf16),
            pltpu.VMEM((units, 2 * n_tok), bf16),
            pltpu.VMEM((units, 2 * n_tok), bf16),
            dma((3,)),
            dma((2, 4)), dma((4,)),
            dma((4,)), dma((4,)), dma((4,)), dma((4,)),
            dma((4,)), dma((4,)), dma((4,)), dma((4,)),
            dma((4, 4)), dma((4, 4)),
            dma((2, 4)), dma((4,)),
        ],
        cost_estimate=pl.CostEstimate(
            flops=12 * rows * feats * units, bytes_accessed=12 * feats * units, transcendentals=rows * units
        ),
        compiler_params=pltpu.CompilerParams(
            collective_id=0, has_side_effects=True, vmem_limit_bytes=60 * 1024 * 1024
        ),
    )(tokens.T, grad_out.T, expert_ids.T, probs.T, w_gate[0], w_up[0], w_down[0])
    blocks = [pl.BlockSpec((size // 5, other), lambda i: (i, 0)) for size, other in ((feats, units), (feats, units), (units, feats))]
    outs = pl.pallas_call(
        copy_kernel,
        out_shape=shapes,
        grid=(5,),
        in_specs=blocks,
        out_specs=tuple(blocks),
        cost_estimate=pl.CostEstimate(flops=0, bytes_accessed=12 * feats * units, transcendentals=0),
        compiler_params=pltpu.CompilerParams(vmem_limit_bytes=60 * 1024 * 1024),
    )(*outs)
    return tuple(out[None] for out in outs)


def solution(mesh):
    body = shards
    if mesh.shape["ep"] == 8 and mesh.shape["section"] == 4:
        body = fused
    placed = (
        P("ep", "section"),
        P("ep", "section"),
        P("ep", None),
        P("ep", None),
        P("ep", None, "section"),
        P("ep", None, "section"),
        P("ep", "section", None),
    )
    return jax.shard_map(
        body,
        mesh=mesh,
        in_specs=placed,
        out_specs=(P("ep", None, "section"), P("ep", None, "section"), P("ep", "section", None)),
        check_vma=False,
    )
```

profile of v0, /device:TPU:9, one launch (start us, length us, event | category | flops | bytes accessed | tf_op | source)
XLA Modules:
  0.0 78.1 jit_solution(276331377676138138)
XLA Ops:
  0.6 70.2 %shard_map.94 = (bf16[1440,720]{1,0:T(8,128)(2,1)}, bf16[1440,720]{1,0:T(8,128)(2,1)}, bf16[720,1440]{1,0:T(8,128)(2,1)}) custom-call(bf16[360,256]{1,0:T(8,128)(2,1)} %bitcast.16, bf16[360,256]{1,0:T(8,128)(2,1)} %bitcast.17, s32[4,256]{1,0:T(4,128)} %bitcast.18, f32[4,256]{1,0:T(4,128)} %bitcast.19, bf16[1440,720]{1,0:T(8,128)(2,1)} %bitcast.10, ...), custom_call_target="tpu_custom_call" | custom-call | flops 25480396800 | bytes 12441600 | tf_op jit(solution)/shard_map/pallas_call | solution.py:429
  70.8 7.3 %shard_map.95 = (bf16[1440,720]{1,0:T(8,128)(2,1)}, bf16[1440,720]{1,0:T(8,128)(2,1)}, bf16[720,1440]{1,0:T(8,128)(2,1)}) custom-call(bf16[1440,720]{1,0:T(8,128)(2,1)} %get-tuple-element.9.gate, bf16[1440,720]{1,0:T(8,128)(2,1)} %get-tuple-element.10.up, bf16[720,1440]{1,0:T(8,128)(2,1)} %get-tuple-element.11.down), custom_call_target="tpu_custom_call" | custom-call | bytes 12441600 | tf_op jit(solution)/shard_map/pallas_call | solution.py:464
where the time goes:
time: 78.4 us; the launch traced here: 78.1 us
  Pallas kernels  77.4 us (99%)
    pallas_call x1, Pallas kernels, fused(): pl.pallas_call(fused_kernel, out_shape=shapes, in_specs=[vmem] * 4 + [hbm...  70.2 us
    pallas_call x1, Pallas kernels, fused(): pl.pallas_call(copy_kernel, out_shape=shapes, grid=(5,), in_specs=blocks,...  7.26 us

commit v1 on v0

--- a/solution.py
+++ b/solution.py
@@ -75,9 +75,9 @@
 
 def fused_kernel(
     tokens, grad_out, ids, probs, w_gate, w_up, w_down,
-    out_gate, out_up, out_down,
+    out_gate, out_up, out_down, out_in, out_scaled, out_term_gate, out_term_linear, out_term_hidden,
     held, wg, wu, wd, wg_t, wu_t, acc_gate, acc_up, acc_down, cols_in, cols_scaled, term_gate, term_linear, term_hidden,
-    w_sem, z_send, z_recv, x_send, x_recv, y_send, y_recv, dx_send, dx_recv, dy_send, dy_recv, c_send, c_recv, d_send, d_recv,
+    part_gate, part_up, part_down, out_sem, w_sem, z_send, z_recv, x_send, x_recv, y_send, y_recv, dx_send, dx_recv, dy_send, dy_recv, c_send, c_recv, d_send, d_recv,
 ):
     sec, me = lax.axis_index("section"), lax.axis_index("ep")
     width, n_tok = tokens.shape
@@ -299,6 +299,25 @@
         wg_t[:, at:to] = wg[at:to, :].T
         wu_t[:, at:to] = wu[at:to, :].T
 
+    def finish(m, carry):
+        part = feats // 6
+        here = pl.ds(pl.multiple_of(m * part, 16), part)
+        part_gate[here, :] = acc_gate[here, :].astype(jnp.bfloat16)
+        part_up[here, :] = acc_up[here, :].astype(jnp.bfloat16)
+        return carry
+
+    def finish_down(m, carry):
+        part = units // 3
+        here = pl.ds(pl.multiple_of(m * part, 16), part)
+        part_down[here, :] = acc_down[here, :].astype(jnp.bfloat16)
+        return carry
+
+    pairs = (
+        (part_gate, out_gate), (part_up, out_up), (part_down, out_down), (cols_in, out_in), (cols_scaled, out_scaled),
+        (term_gate, out_term_gate), (term_linear, out_term_linear), (term_hidden, out_term_hidden),
+    )
+    results = [pltpu.make_async_copy(src, dst, out_sem.at[i]) for i, (src, dst) in enumerate(pairs)]
+
     def step(k, carry):
         x_arrived(k)
         by_step(k, lambda first: y_half(k, first).start())
@@ -355,28 +374,23 @@
             d_arrived(3)
             d_out(3, 3).start()
 
-        weights()
+        @pl.when(k < 3)
+        def _():
+            weights()
+
+        @pl.when(k == 2)
+        def _():
+            lax.fori_loop(0, 6, finish, 0)
+            lax.fori_loop(0, 3, finish_down, 0)
+            for result in results[:3]:
+                result.start()
+
         return carry
 
     lax.fori_loop(0, 4, step, 0)
 
-    def finish(m, carry):
-        part = feats // 6
-        here = pl.ds(pl.multiple_of(m * part, 16), part)
-        out_gate[here, :] = acc_gate[here, :].astype(jnp.bfloat16)
-        out_up[here, :] = acc_up[here, :].astype(jnp.bfloat16)
-        return carry
-
-    lax.fori_loop(0, 6, finish, 0)
-
-    def finish_down(m, carry):
-        part = units // 3
-        here = pl.ds(pl.multiple_of(m * part, 16), part)
-        out_down[here, :] = acc_down[here, :].astype(jnp.bfloat16)
-        return carry
-
-    lax.fori_loop(0, 3, finish_down, 0)
-
+    for result in results[3:]:
+        result.start()
     z_in(0, 1 + zz).wait_send()
     d_in(0, 1 + zz).wait_send()
 
@@ -405,12 +419,22 @@
         return carry
 
     lax.fori_loop(0, 4, drain, 0)
-
-
-def copy_kernel(gate, up, down, out_gate, out_up, out_down):
-    out_gate[...] = gate[...]
-    out_up[...] = up[...]
-    out_down[...] = down[...]
+    for result in results:
+        result.wait()
+
+
+def last_kernel(
+    part_gate, part_up, part_down, cols_in, cols_scaled, term_gate, term_linear, term_hidden, out_gate, out_up, out_down
+):
+    def outer(lhs, rhs):
+        return lax.dot_general(lhs, rhs, (((1,), (1,)), ((), ())), preferred_element_type=jnp.float32)
+
+    for part, out, lhs, rhs in (
+        (part_gate, out_gate, cols_in, term_gate),
+        (part_up, out_up, cols_in, term_linear),
+        (part_down, out_down, term_hidden, cols_scaled),
+    ):
+        out[...] = (part[...].astype(jnp.float32) + outer(lhs[...], rhs[...])).astype(jnp.bfloat16)
 
 
 def fused(tokens, grad_out, expert_ids, probs, w_gate, w_up, w_down):
@@ -428,9 +452,10 @@
     )
     outs = pl.pallas_call(
         fused_kernel,
-        out_shape=shapes,
+        out_shape=shapes
+        + tuple(jax.ShapeDtypeStruct((size, 2 * n_tok), bf16) for size in (feats, feats, units, units, units)),
         in_specs=[vmem] * 4 + [hbm] * 3,
-        out_specs=(vmem,) * 3,
+        out_specs=(hbm,) * 8,
         scratch_shapes=[
             pltpu.VMEM((n_ep, n_sec, 2 * width + 2 * n_ep, n_tok), bf16),
             pltpu.VMEM((feats, units), bf16),
@@ -446,6 +471,10 @@
             pltpu.VMEM((units, 2 * n_tok), bf16),
             pltpu.VMEM((units, 2 * n_tok), bf16),
             pltpu.VMEM((units, 2 * n_tok), bf16),
+            pltpu.VMEM((feats, units), bf16),
+            pltpu.VMEM((feats, units), bf16),
+            pltpu.VMEM((units, feats), bf16),
+            dma((8,)),
             dma((3,)),
             dma((2, 4)), dma((4,)),
             dma((4,)), dma((4,)), dma((4,)), dma((4,)),
@@ -460,14 +489,25 @@
             collective_id=0, has_side_effects=True, vmem_limit_bytes=60 * 1024 * 1024
         ),
     )(tokens.T, grad_out.T, expert_ids.T, probs.T, w_gate[0], w_up[0], w_down[0])
-    blocks = [pl.BlockSpec((size // 5, other), lambda i: (i, 0)) for size, other in ((feats, units), (feats, units), (units, feats))]
+    steps = 5
+
+    def by_rows(size, other):
+        return pl.BlockSpec((size // steps, other), lambda i: (i, 0))
+
+    def whole(size):
+        return pl.BlockSpec((size, 2 * n_tok), lambda i: (0, 0))
+
+    blocks = [by_rows(feats, units), by_rows(feats, units), by_rows(units, feats)]
     outs = pl.pallas_call(
-        copy_kernel,
+        last_kernel,
         out_shape=shapes,
-        grid=(5,),
-        in_specs=blocks,
+        grid=(steps,),
+        in_specs=blocks
+        + [by_rows(feats, 2 * n_tok), whole(feats), whole(units), whole(units), by_rows(units, 2 * n_tok)],
         out_specs=tuple(blocks),
-        cost_estimate=pl.CostEstimate(flops=0, bytes_accessed=12 * feats * units, transcendentals=0),
+        cost_estimate=pl.CostEstimate(
+            flops=12 * n_tok * feats * units, bytes_accessed=12 * feats * units, transcendentals=0
+        ),
         compiler_params=pltpu.CompilerParams(vmem_limit_bytes=60 * 1024 * 1024),
     )(*outs)
     return tuple(out[None] for out in outs)

time: 78.4 us -> 77.5 us (0.989)
  no operation moved by 1% of the time
where the time goes in v1:
time: 77.5 us; the launch traced here: 77.3 us
  Pallas kernels  76.7 us (99%)
    pallas_call x1, Pallas kernels, fused(): pl.pallas_call(fused_kernel, out_shape=shapes + tuple((jax.ShapeDtypeStru...  66.2 us
    pallas_call x1, Pallas kernels, fused(): pl.pallas_call(last_kernel, out_shape=shapes, grid=(steps,), in_specs=blo...  10.4 us

profile of v1, /device:TPU:9, one launch (start us, length us, event | category | flops | bytes accessed | tf_op | source)
XLA Modules:
  0.0 77.3 jit_solution(12067406047738322317)
XLA Ops:
  0.6 66.2 %shard_map.94 = (bf16[1440,720]{1,0:T(8,128)(2,1)}, bf16[1440,720]{1,0:T(8,128)(2,1)}, bf16[720,1440]{1,0:T(8,128)(2,1)}, bf16[1440,512]{1,0:T(8,128)(2,1)}, bf1...) custom-call(bf16[360,256]{1,0:T(8,128)(2,1)} %bitcast.16, ...), custom_call_target="tpu_custom_call" | custom-call | flops 25480396800 | bytes 12441600 | tf_op jit(solution)/shard_map/pallas_call | solution.py:453
  66.9 10.4 %shard_map.95 = (bf16[1440,720]{1,0:T(8,128)(2,1)}, bf16[1440,720]{1,0:T(8,128)(2,1)}, bf16[720,1440]{1,0:T(8,128)(2,1)}) custom-call(bf16[1440,720]{1,0:T(8,128)(2,1)} %get-tuple-element.14.part_gate, bf16[1440,720]{1,0:T(8,128)(2,1)} %get-tuple-element.15.part_up, bf16[720,1440]{1,0:T(8,128)(2,1)} %get-tuple-element.16.part_down, ...), custom_call_target="tpu_custom_call" | custom-call | flops 3185049600 | bytes 12441600 | tf_op jit(solution)/shard_map/pallas_call | solution.py:501
